TPU v7x, 32 devices: a whole 2x2x4 slice. The times are simulated.
32 devices in a mesh: ctx: 4 (over y, x), tp: 8 (over z, core).
Axes of the slice: x: 2, y: 2, z: 4, core: 2. Of those that a mesh axis runs over, the one named last changes fastest.
Arguments:
- x_input: bfloat16 [1024, 4096], P('ctx', 'tp'), may hold values from -6 to 6
- z_input: bfloat16 [1024, 4096], P('ctx', 'tp'), may hold values from -6 to 6
- bc_input: bfloat16 [1024, 1024], P('ctx', 'tp'), may hold values from -6 to 6
- dt_input: float32 [1024, 64], P('ctx', 'tp'), may hold values from -6 to 6
- decay_log: float32 [64], P('tp'), may hold values from -12 to -2
- skip_weight: float32 [64], P('tp'), may hold values from 0.5 to 2
- conv_x: float32 [4, 4096], P(None, 'tp'), may hold values from -3 to 3
- conv_bc: float32 [4, 1024], replicated, may hold values from -3 to 3
- conv_bias_x: float32 [4096], P('tp'), may hold values from -3 to 3
- conv_bias_bc: float32 [1024], replicated, may hold values from -3 to 3
- norm_gain: float32 [4096], P('tp'), may hold values from 0.1 to 1.9
- out_weight: bfloat16 [4096, 8192], P('tp'), may hold values from -0.09375 to 0.09375
Outputs:
- mixed: bfloat16 [1024, 8192], P('ctx', 'tp')
All inputs are finite; a program needn't handle non-finite values.
Results may differ from a plain program's by a relative error of at most 0.0055.
Values may be sent and summed in bfloat16 or wider, within the bound.
A program may use at most 128 MiB of HBM per device.

v0:
```python
import jax
import jax.numpy as jnp
from jax import lax
from jax.sharding import PartitionSpec as P

HIGH = lax.Precision.HIGHEST


def from_behind(value, axis, steps):
    count = lax.axis_size(axis)
    initial, last = (max(0, -steps), min(count, count - steps))
    return lax.ppermute(value, axis, [(source, source + steps) for source in range(initial, last)])


def swapped(value, axis, distance):
    mask = 2**distance
    pairs = [(source, source ^ mask) for source in range(lax.axis_size(axis))]
    return lax.ppermute(value, axis, pairs)


def prefix(part, axis, combine, identity):
    place = lax.axis_index(axis)
    gathered = jax.tree.map(lambda a: lax.all_gather(a, axis), part)
    state = jax.tree.map(lambda a, e: jnp.zeros_like(a) + jnp.asarray(e, a.dtype), part, identity)

    def one(turn, state):
        return combine(
            state, jax.tree.map(lambda a: lax.dynamic_index_in_dim(a, turn, 0, False), gathered)
        )

    return lax.fori_loop(0, place, one, state)


def causal_conv(previous, current, kernel, offset):
    joined = jnp.concatenate([previous.astype(jnp.float32), current.astype(jnp.float32)], axis=0)
    length = current.shape[0]
    total = offset[None, :] + kernel[0][None, :] * joined[0:length]
    for step in range(1, kernel.shape[0]):
        total = total + kernel[step][None, :] * joined[step : step + length]
    return jax.nn.silu(total)


def chain_combine(earlier, later_part):
    return (earlier[0] * later_part[0], later_part[0] * earlier[1] + later_part[1])


def shards(
    x_input,
    z_input,
    bc_input,
    dt_input,
    decay_log,
    skip_weight,
    conv_x,
    conv_bc,
    conv_bias_x,
    conv_bias_bc,
    norm_gain,
    out_weight,
):
    length = x_input.shape[0]
    inner = x_input.shape[1]
    state_size = bc_input.shape[1]
    heads = dt_input.shape[1]
    head_size = inner // heads
    reach = conv_x.shape[0] - 1
    rank = lax.axis_index("tp")
    odd = rank % 2 == 1
    raw = jnp.concatenate([x_input, bc_input], axis=1)
    own_start = rank * state_size
    kernel = jnp.concatenate(
        [conv_x, lax.dynamic_slice_in_dim(conv_bc, own_start, state_size, 1)], axis=1
    )
    offset = jnp.concatenate(
        [conv_bias_x, lax.dynamic_slice_in_dim(conv_bias_bc, own_start, state_size, 0)], axis=0
    )
    tails = from_behind(raw[length - reach :], "ctx", 1)
    conv_out = causal_conv(tails, raw, kernel, offset)
    xs = conv_out[:, :inner]
    own_half = conv_out[:, inner:]
    other_half = swapped(own_half, "tp", 0)
    b_mat = jnp.where(odd, other_half, own_half)
    c_mat = jnp.where(odd, own_half, other_half)
    step_size = jax.nn.softplus(dt_input)
    decay_rate = -jnp.exp(decay_log)
    running = jnp.cumsum(step_size * decay_rate[None, :], axis=0)
    heads_x = xs.reshape(length, heads, head_size)
    intersection = jnp.dot(c_mat, b_mat.T, precision=HIGH)
    lower = jnp.tril(jnp.ones((length, length), dtype=bool))
    gap = running.T[:, :, None] - running.T[:, None, :]
    weights = (
        jnp.where(lower[None], jnp.exp(jnp.minimum(gap, 0.0)), 0.0)
        * intersection[None]
        * step_size.T[:, None, :]
    )
    local_out = jnp.einsum("hts,shp->thp", weights, heads_x, precision=HIGH)
    closing = jnp.exp(running[-1][None, :] - running) * step_size
    local_state = jnp.einsum("sh,shp,sn->hpn", closing, heads_x, b_mat, precision=HIGH)
    passing = jnp.exp(running[-1])[:, None, None]
    prefix_decay, incoming = prefix(
        (passing, local_state),
        "ctx",
        chain_combine,
        (jnp.ones_like(passing), jnp.zeros_like(local_state)),
    )
    carried = (
        jnp.einsum("tn,hpn->thp", c_mat, incoming, precision=HIGH) * jnp.exp(running)[:, :, None]
    )
    ssm_out = local_out + carried + skip_weight[None, :, None] * heads_x
    gated = ssm_out.reshape(length, inner) * jax.nn.silu(z_input.astype(jnp.float32))
    squares = jnp.sum(gated * gated, axis=1)
    hidden = (gated * norm_gain[None, :]).astype(jnp.bfloat16)
    total_squares = lax.psum(squares, "tp")
    scale = lax.rsqrt(total_squares / (inner * lax.axis_size("tp")) + 1e-05)
    reduced = lax.psum_scatter(
        lax.dot_general(
            out_weight, hidden, (((0,), (1,)), ((), ())), preferred_element_type=jnp.float32
        ),
        "tp",
        scatter_dimension=0,
        tiled=True,
    )
    return (reduced.T * scale[:, None]).astype(jnp.bfloat16)


def solution(mesh):
    in_specs = (
        P("ctx", "tp"),
        P("ctx", "tp"),
        P("ctx", "tp"),
        P("ctx", "tp"),
        P("tp"),
        P("tp"),
        P(None, "tp"),
        P(),
        P("tp"),
        P(),
        P("tp"),
        P("tp", None),
    )
    out_specs = P("ctx", "tp")
    return jax.shard_map(shards, mesh=mesh, in_specs=in_specs, out_specs=out_specs, check_vma=False)
```

profile of v0, /device:TPU:0, one launch (start us, length us, event | category | flops | bytes accessed | tf_op | source)
XLA Modules:
  0.0 160.6 jit_solution(4837453477676947085)
XLA Ops:
  6.5 0.0 copy-start
  6.5 0.0 copy-start.3
  6.5 0.0 all-gather.5.cloned.1.call-start
  6.5 1.0 constant_dynamic-update-slice_fusion.1
  7.5 0.9 constant_dynamic-update-slice_fusion
  8.4 4.8 %collective-permute-start = (bf16[3,640]{1,0:T(4,128)(2,1)S(1)}, bf16[3,640]{1,0:T(4,128)(2,1)S(1)}, u32[]{:S(2)}, u32[]{:S(2)}) collective-permute-start(bf16[3,640]{1,0:T(4,128)(2,1)S(1)} %slice.55), channel_id=1, source_target_pairs={{0,8},{8,16},{16,24},{1,9},{9,17},{17,25},{2,10},{10,18},{18,26},{... | collective-permute-start | bytes 11528 | tf_op jit(solution)/shard_map/ppermute | solution.py:12
  13.3 0.7 exponential_negate_fusion
  13.9 0.8 multiply_bitcast_fusion
  14.7 0.6 reduce-window.6
  15.3 0.2 slice_reduce_fusion
  15.5 0.1 fusion.52
  15.5 0.2 slice_reduce_fusion.1
  15.7 0.8 dynamic_slice.16
  16.5 0.7 pad_maximum_fusion.1
  17.2 0.0 copy-done
  17.3 0.9 fusion.44
  18.2 0.0 collective-permute-done
  18.2 0.4 divide_multiply_fusion
  18.6 0.1 collective-permute-start.1
  18.7 0.0 copy-done.3
  18.7 0.1 exponential_multiply_fusion
  18.8 0.1 slice.64
  18.9 0.2 copy.19
  19.1 1.0 collective-permute-done.1
  20.1 1.3 fusion.32
  21.3 0.0 all-gather.5.cloned.1.call-update
  21.4 0.0 reduce-scatter.2.cloned.1.call-start
  21.4 7.9 %all-gather.2 = f32[4,1,8]{2,1,0:T(1,128)S(1)} all-gather(f32[1,1,8]{2,1,0:T(1,128)S(1)} %bitcast.47), channel_id=2, replica_groups=mesh['ctx'=4,'tp'=8] {'ctx'}, dimensions={0}, use_global_device_ids=true | all-gather | bytes 160 | tf_op jit(solution)/shard_map/all_gather | solution.py:23
  29.4 0.1 add_bitcast_fusion.1
  29.4 0.4 fusion.38
  29.8 2.6 %fusion.9 = f32[256,8,64]{0,2,1:T(8,128)S(1)} fusion(f32[256,8,64]{0,2,1:T(8,128)S(1)} %bitcast.43, f32[8,256]{1,0:T(8,128)S(1)} %get-tuple-element.84, f32[256,256]{1,0:T(8,128)S(1)} %fusion.38, f32[8,256]{1,0:T(8,128)S(1)} %add_bitcast_fusion.1, pred[256,256]{1,0:T(8,128)(4,1)S(1)} %iota_compare_fusion), kind=kOutput, calls=%fused_computation.13 | convolution fusion | flops 405274624 | bytes 1392640 | tf_op jit(solution)/shard_map/hts,shp->thp/dot_general | solution.py:96
  32.4 16.1 %all-gather.5.cloned.1.call-done = f32[32,64,128]{2,1,0:T(8,128)} async-done(((f32[8,64,128]{2,1,0:T(8,128)}), f32[32,64,128]{2,1,0:T(8,128)}) %all-gather.5.cloned.1.call-update) | async-done | bytes 1048592 | tf_op jit(solution)/shard_map/all_gather | solution.py:23
  48.5 0.0 copy-start.4
  48.5 0.0 copy-start.1
  48.5 0.0 copy-start.2
  48.6 0.6 copy-done.4
  49.2 0.6 fusion.8
  49.7 0.2 copy.21
  50.0 0.0 copy-done.1
  50.0 0.0 copy-done.2
  50.0 9.0 %convolution_bitcast_fusion = f32[8192,256]{0,1:T(8,128)} fusion(bf16[512,8192]{1,0:T(8,128)(2,1)} %param.25, f32[512]{0:T(512)S(1)} %copy-done.2, f32[256,512]{1,0:T(8,128)S(1)} %copy.21, bf16[256,512]{1,0:T(8,128)(2,1)S(1)} %copy-done.1), kind=kOutput, calls=%fused_computation.2 | convolution fusion | flops 2148532224 | bytes 17565696 | tf_op jit(solution)/shard_map/dot_general | solution.py:116
  59.0 0.0 reduce-scatter.2.cloned.1.call-update
  59.0 0.2 multiply_reduce_fusion
  59.3 16.5 %psum.7 = f32[256]{0:T(256)S(1)} all-reduce(f32[256]{0:T(256)S(1)} %multiply_reduce_fusion), channel_id=1, replica_groups=mesh['ctx'=4,'tp'=8] {'tp'}, use_global_device_ids=true, to_apply=%region_6.7 | all-reduce | flops 256 | bytes 2048 | tf_op jit(solution)/shard_map/psum | solution.py:113
  75.7 75.9 %reduce-scatter.2.cloned.1.call-done = f32[1024,256]{0,1:T(8,128)} async-done(((f32[8192,256]{0,1:T(8,128)}), f32[1024,256]{0,1:T(8,128)}) %reduce-scatter.2.cloned.1.call-update) | async-done | bytes 1048592 | tf_op jit(solution)/shard_map/reduce_scatter | solution.py:115
  151.6 2.1 %fusion.31 = bf16[256,1024]{1,0:T(8,128)(2,1)} fusion(f32[1024,256]{0,1:T(8,128)} %reduce-scatter.2.cloned.1.call-done, f32[256]{0:T(256)S(1)} %add_rsqrt_fusion), kind=kLoop, calls=%fused_computation.40 | loop fusion | flops 524288 | bytes 1573888 | tf_op jit(solution)/shard_map/convert_element_type | solution.py:123
  (11 shorter events, 0.2 us)
Async XLA Ops:
  6.5 10.7 %copy-start = (f32[4,1024]{1,0:T(4,128)S(1)}, f32[4,1024]{1,0:T(4,128)}, u32[]{:S(2)}) copy-start(f32[4,1024]{1,0:T(4,128)} %param.21) | copy-start | bytes 49156
  6.5 12.2 %copy-start.3 = (f32[256,8]{0,1:T(8,128)S(1)}, f32[256,8]{0,1:T(8,128)}, u32[]{:S(2)}) copy-start(f32[256,8]{0,1:T(8,128)} %param.17) | copy-start | bytes 24580
  6.5 41.9 %all-gather.5.cloned.1.call-start = ((), (), s32[]{:S(2)}) async-start(), calls=%async_computation.2 | async-start | bytes 1310720 | tf_op jit(solution)/shard_map/all_gather | solution.py:23
  8.4 9.8 %collective-permute-start = (bf16[3,640]{1,0:T(4,128)(2,1)S(1)}, bf16[3,640]{1,0:T(4,128)(2,1)S(1)}, u32[]{:S(2)}, u32[]{:S(2)}) collective-permute-start(bf16[3,640]{1,0:T(4,128)(2,1)S(1)} %slice.55), channel_id=1, source_target_pairs={{0,8},{8,16},{16,24},{1,9},{9,17},{17,25},{2,10},{10,18},{18,26},{... | collective-permute-start | bytes 11528 | tf_op jit(solution)/shard_map/ppermute | solution.py:12
  18.6 1.4 collective-permute-start.1
  21.4 130.3 %reduce-scatter.2.cloned.1.call-start = ((), (), s32[]{:S(2)}) async-start(), calls=%async_computation.1 | async-start | bytes 9437184 | tf_op jit(solution)/shard_map/reduce_scatter | solution.py:115
  48.5 0.7 copy-start.4
  48.5 1.4 copy-start.1
  48.5 1.4 copy-start.2
Sparse Core Ops, SparseCore 0:
  21.5 26.9 all-gather.4
  59.1 92.4 reduce-scatter.1
where the time goes:
time: 161 us
  waiting for transfers between devices  93 us (58%)
  blocking collectives  24.4 us (15%)
  matrix products  13.8 us (9%)
  between operations  13.6 us (8%)
  other arithmetic  6.72 us (4%)
  starting transfers between devices  4.96 us (3%)
  local copies, waits for them, and re-layouts  4.1 us (3%)
    reduce_scatter x1, waiting for transfers between devices, shards(): lax.psum_scatter(lax.dot_general(out_weight, hidden, (((0,), (1,)), ((),...  75.9 us
    psum x1, blocking collectives, shards(): total_squares = lax.psum(squares, 'tp')  16.5 us
    all_gather x1, waiting for transfers between devices, prefix(): gathered = jax.tree.map(lambda a: lax.all_gather(a, axis), part)  16.1 us
    dot_general x1, matrix products, shards(): lax.dot_general(out_weight, hidden, (((0,), (1,)), ((), ())), preferred_e...  9.01 us
    all_gather x1, blocking collectives, prefix(): gathered = jax.tree.map(lambda a: lax.all_gather(a, axis), part)  7.93 us
    ppermute x1, starting transfers between devices, from_behind(): lax.ppermute(value, axis, [(source, source + steps) for source in range(i...  4.84 us
  transfers between devices with their start and end apart: 4, of which 3 were waited for; matrix products, arithmetic and copies ran while one was open for 5% of the time, Pallas kernels for 0%

commit v1 on v0

v1 whole, which is shorter than its diff:
```python
import functools

import jax
import jax.numpy as jnp
from jax import lax
from jax.experimental import pallas as pl
from jax.experimental.pallas import tpu as pltpu
from jax.sharding import PartitionSpec as P

MESH = pl.DeviceIdType.MESH
HIGH = lax.Precision.HIGHEST
F32 = jnp.float32
BF16 = jnp.bfloat16
HALO = 16
CHUNKS = 4


def dot(a, b, precision=None):
    return jnp.dot(a, b, preferred_element_type=F32, precision=precision)


def silu(v):
    return v / (1.0 + jnp.exp(-v))


def split(v):
    high = v.astype(BF16)
    return high, (v - high.astype(F32)).astype(BF16)


def layer_kernel(
    n_ctx,
    n_tp,
    x_ref,
    z_ref,
    bc_ref,
    dt_ref,
    decay_ref,
    skip_ref,
    conv_x_ref,
    conv_bc_ref,
    bias_x_ref,
    bias_bc_ref,
    gain_ref,
    w_ref,
    out_ref,
    halo_x,
    halo_bc,
    raw_bc,
    pad_x,
    pad_bc,
    xs,
    y,
    grown,
    state_own,
    carry_own,
    state_in,
    carry_in,
    incoming,
    squares,
    hid_own,
    hid_sib,
    w_own,
    w_sib,
    acc,
    outgoing,
    arrived,
    halo_send,
    halo_recv,
    state_send,
    state_recv,
    square_send,
    square_recv,
    hid_sem,
    w_local,
    w_send,
    w_recv,
    block_send,
    block_recv,
):
    ctx = lax.axis_index("ctx")
    rank = lax.axis_index("tp")
    zed = rank // 2
    core = rank % 2
    sib = rank + 1 - 2 * core
    n_z = n_tp // 2
    length, inner = x_ref.shape
    size = bc_ref.shape[1]
    heads = dt_ref.shape[1]
    taps = conv_x_ref.shape[0]
    width = w_own.shape[2]
    rows = length // CHUNKS
    wide = 2 * (inner // heads)

    barrier = pltpu.get_barrier_semaphore()

    def greet(c, r):
        pl.semaphore_signal(barrier, inc=1, device_id=(c, r), device_id_type=MESH)

    for step in range(1, n_tp):
        greet(ctx, lax.rem(rank + step, n_tp))
    for step in range(1, n_ctx):
        greet(lax.rem(ctx + step, n_ctx), rank)
    greet(lax.rem(ctx + 1, n_ctx), sib)
    greet(lax.rem(ctx + n_ctx - 1, n_ctx), sib)

    def w_block(block, half):
        return w_ref.at[:, pl.ds(pl.multiple_of((2 * block + half) * width, width), width)]

    def remote(src, dst, send, recv, c, r):
        return pltpu.make_async_remote_copy(
            src_ref=src,
            dst_ref=dst,
            send_sem=send,
            recv_sem=recv,
            device_id=(c, r),
            device_id_type=MESH,
        )

    local_w = [
        pltpu.make_async_copy(w_block(b, core), w_own.at[b], w_local.at[b]) for b in range(n_z)
    ]
    pl.semaphore_wait(barrier, (n_tp - 1) + (n_ctx - 1) + 2)

    later = lax.rem(ctx + 1, n_ctx)
    tail = pl.ds(length - HALO, HALO)
    x_halo = remote(
        x_ref.at[tail], halo_x, halo_send.at[0], halo_recv.at[0], later, rank
    )
    bc_halo = remote(
        bc_ref.at[tail], halo_bc.at[core], halo_send.at[1], halo_recv.at[1 + core], later, rank
    )
    bc_halo_sib = remote(
        bc_ref.at[tail], halo_bc.at[core], halo_send.at[2], halo_recv.at[1 + core], later, sib
    )
    bc_swap = remote(
        bc_ref, raw_bc.at[core], halo_send.at[3], halo_recv.at[3], ctx, sib
    )

    @pl.when(ctx < n_ctx - 1)
    def _():
        x_halo.start()
        bc_halo.start()
        bc_halo_sib.start()

    bc_swap.start()
    sent_w = [
        remote(w_block(b, 1 - core), w_sib.at[b], w_send.at[b], w_recv.at[b], ctx, sib)
        for b in range(n_z)
    ]
    for b in range(n_z):
        sent_w[b].start()
        local_w[b].start()
    raw_bc[core] = bc_ref[...]

    logits = dt_ref[...].T
    step_size = jnp.maximum(logits, 0.0) + jnp.log(1.0 + jnp.exp(-jnp.abs(logits)))
    rate = -jnp.exp(decay_ref[...])
    earlier = lax.broadcasted_iota(jnp.int32, (length, length), 0)
    after = lax.broadcasted_iota(jnp.int32, (length, length), 1)
    upper = jnp.where(earlier <= after, 1.0, 0.0).astype(F32)
    running = dot(step_size * rate, upper, HIGH)
    total = running[:, length - 1 : length]
    closing = jnp.exp(total - running) * step_size
    running_col = running.T
    closing_col = closing.T
    grown_col = jnp.exp(running_col)
    last_col = grown_col[length - 1 : length, :]
    lane = lax.broadcasted_iota(jnp.int32, (1, wide), 1)
    first = lane < wide // 2

    def spread(cols, pair):
        return jnp.where(
            first, cols[:, 2 * pair : 2 * pair + 1], cols[:, 2 * pair + 1 : 2 * pair + 2]
        )

    pairs = heads // 2
    for p in range(pairs):
        at = slice(p * wide, (p + 1) * wide)
        grown[:, at] = spread(grown_col, p)
        carry_own[:, at] = jnp.broadcast_to(spread(last_col, p), (8, wide))

    @pl.when(ctx == 0)
    def _():
        halo_x[...] = jnp.zeros_like(halo_x)
        halo_bc[...] = jnp.zeros_like(halo_bc)

    @pl.when(ctx > 0)
    def _():
        x_halo.wait_recv()

    def conv(pad, kernel, bias):
        value = bias
        for k in range(taps):
            start = HALO - (taps - 1) + k
            value = value + kernel[k : k + 1, :] * pad[start : start + length, :]
        return silu(value)

    pad_x[0:HALO, :] = halo_x[...].astype(F32)
    pad_x[HALO:, :] = x_ref[...].astype(F32)
    xs[...] = conv(pad_x, conv_x_ref[...], bias_x_ref[...])

    @pl.when(ctx > 0)
    def _():
        for half in range(2):
            pltpu.make_async_copy(
                halo_bc.at[half], halo_bc.at[half], halo_recv.at[1 + half]
            ).wait()

    bc_swap.wait_recv()
    for half in range(2):
        at = slice(half * size, (half + 1) * size)
        pad_bc[0:HALO, at] = halo_bc[half].astype(F32)
        pad_bc[HALO:, at] = raw_bc[half].astype(F32)
    group = pl.ds(pl.multiple_of(zed * 2 * size, 2 * size), 2 * size)
    bcs = conv(pad_bc, conv_bc_ref[:, group], bias_bc_ref[:, group])
    b_mat = bcs[:, :size]
    c_mat = bcs[:, size:]

    b_turned = b_mat.T.astype(BF16)
    for p in range(pairs):
        at = slice(p * wide, (p + 1) * wide)
        scaled = (xs[:, at] * spread(closing_col, p)).astype(BF16)
        state_own[:, at] = dot(b_turned, scaled).astype(BF16)

    def state_copies(target):
        return (
            remote(
                state_own,
                state_in.at[ctx],
                state_send.at[0, target],
                state_recv.at[0, ctx],
                target,
                rank,
            ),
            remote(
                carry_own,
                carry_in.at[ctx],
                state_send.at[1, target],
                state_recv.at[1, ctx],
                target,
                rank,
            ),
        )

    for target in range(1, n_ctx):

        @pl.when(target > ctx)
        def _():
            for copy in state_copies(target):
                copy.start()

    meeting = lax.dot_general(
        c_mat, b_mat, (((1,), (1,)), ((), ())), preferred_element_type=F32, precision=HIGH
    )
    meeting = jnp.where(earlier >= after, meeting, 0.0)
    for p in range(pairs):
        at = slice(p * wide, (p + 1) * wide)
        values = xs[:, at]
        high, low = split(values)
        both = jnp.concatenate([high, low], axis=1)
        parts = []
        for h in (2 * p, 2 * p + 1):
            gap = running_col[:, h : h + 1] - running[h : h + 1, :]
            weights = jnp.exp(jnp.minimum(gap, 0.0)) * meeting * step_size[h : h + 1, :]
            product = dot(weights.astype(BF16), both)
            parts.append(product[:, :wide] + product[:, wide:])
        y[:, at] = jnp.where(first, parts[0], parts[1]) + values * jnp.where(
            first, skip_ref[0, 2 * p], skip_ref[0, 2 * p + 1]
        )
    gate = silu(z_ref[...].astype(F32))

    incoming[...] = jnp.zeros_like(incoming)
    for source in range(n_ctx - 1):

        @pl.when(source < ctx)
        def _():
            pltpu.make_async_copy(
                state_in.at[source], state_in.at[source], state_recv.at[0, source]
            ).wait()
            pltpu.make_async_copy(
                carry_in.at[source], carry_in.at[source], state_recv.at[1, source]
            ).wait()
            incoming[...] = incoming[...] * carry_in[source, 0:1, :] + state_in[source].astype(F32)

    c_high, c_low = split(c_mat)
    state = incoming[...].astype(BF16)
    carried = dot(
        jnp.concatenate([c_high, c_low], axis=1), jnp.concatenate([state, state], axis=0)
    )
    gated = (y[...] + carried * grown[...]) * gate
    hid_own[...] = (gated * gain_ref[...]).astype(BF16)
    hid_swap = remote(hid_own, hid_sib, hid_sem.at[0], hid_sem.at[1], ctx, sib)
    hid_swap.start()
    norm = jnp.sum(gated * gated, axis=1, keepdims=True)
    squares[rank] = jnp.broadcast_to(norm, (length, 128)).T[0:8, :]

    def square_copy(target):
        return remote(
            squares.at[rank],
            squares.at[rank],
            square_send.at[target],
            square_recv.at[rank],
            ctx,
            target,
        )

    for target in range(n_tp):

        @pl.when(target != rank)
        def _():
            square_copy(target).start()

    def part(r):
        return pl.ds(r * rows, rows)

    def block_copy(target, r, forward):
        if forward:
            slot, to = target, rank + 2
        else:
            slot, to = jnp.where(target == zed - 1, n_z, target), rank - 2
        return remote(
            outgoing.at[target, part(r)],
            arrived.at[slot, part(r)],
            block_send.at[target, r],
            block_recv.at[slot, r],
            ctx,
            to,
        )

    def block_wait(slot, r):
        pltpu.make_async_copy(
            arrived.at[slot, part(r)], arrived.at[slot, part(r)], block_recv.at[slot, r]
        ).wait()

    for b in range(n_z):
        local_w[b].wait()
        sent_w[b].wait_recv()
    hid_swap.wait_recv()

    upward = zed < n_z // 2
    for i in range(n_z):
        target = jnp.where(upward, n_z - 1 - i, i)
        total_block = dot(hid_own[...], w_own[target]) + dot(hid_sib[...], w_sib[target])
        acc[target] = total_block

        if i < n_z - 1:

            @pl.when((zed == 0) | (zed == n_z - 1))
            def _():
                outgoing[target] = acc[target].astype(BF16)

            @pl.when(zed == 0)
            def _():
                for r in range(CHUNKS):
                    block_copy(target, r, True).start()

            @pl.when(zed == n_z - 1)
            def _():
                for r in range(CHUNKS):
                    block_copy(target, r, False).start()

    def relay(target, r, forward):
        block_wait(target, r)
        outgoing[target, part(r)] = (
            acc[target, part(r)] + arrived[target, part(r)].astype(F32)
        ).astype(BF16)
        block_copy(target, r, forward).start()

    for i in range(n_z - 1):
        for r in range(CHUNKS):

            @pl.when((zed > 0) & (zed < n_z - 1 - i))
            def _():
                relay(n_z - 1 - i, r, True)

            @pl.when((zed < n_z - 1) & (zed > i))
            def _():
                relay(i, r, False)

    for target in range(n_tp):

        @pl.when(target != rank)
        def _():
            pltpu.make_async_copy(
                squares.at[target], squares.at[target], square_recv.at[target]
            ).wait()

    mean = jnp.sum(squares[...], axis=0) * (1.0 / (inner * n_tp))
    scale = lax.rsqrt(mean + 1e-05).T[:, 0:1]
    for r in range(CHUNKS):

        @pl.when(zed < n_z - 1)
        def _():
            block_wait(n_z, r)
            acc[zed, part(r)] = acc[zed, part(r)] + arrived[n_z, part(r)].astype(F32)

        @pl.when(zed > 0)
        def _():
            block_wait(zed, r)
            acc[zed, part(r)] = acc[zed, part(r)] + arrived[zed, part(r)].astype(F32)

        out_ref[part(r), :] = (
            acc[zed, part(r)] * scale[r * rows : (r + 1) * rows, :]
        ).astype(BF16)

    @pl.when(ctx < n_ctx - 1)
    def _():
        x_halo.wait_send()
        bc_halo.wait_send()
        bc_halo_sib.wait_send()

    bc_swap.wait_send()
    for copy in sent_w:
        copy.wait_send()
    for target in range(1, n_ctx):

        @pl.when(target > ctx)
        def _():
            for copy in state_copies(target):
                copy.wait_send()

    hid_swap.wait_send()
    for target in range(n_tp):

        @pl.when(target != rank)
        def _():
            square_copy(target).wait_send()

    for target in range(n_z):
        for r in range(CHUNKS):

            @pl.when(zed != target)
            def _():
                pltpu.make_async_copy(
                    outgoing.at[target, part(r)],
                    outgoing.at[target, part(r)],
                    block_send.at[target, r],
                ).wait()


def solution(mesh):
    n_ctx, n_tp = mesh.shape["ctx"], mesh.shape["tp"]
    n_z = n_tp // 2

    def shards(
        x_input,
        z_input,
        bc_input,
        dt_input,
        decay_log,
        skip_weight,
        conv_x,
        conv_bc,
        conv_bias_x,
        conv_bias_bc,
        norm_gain,
        out_weight,
    ):
        length, inner = x_input.shape
        size = bc_input.shape[1]
        heads = dt_input.shape[1]
        features = out_weight.shape[1]
        width = features // n_tp
        vmem = pl.BlockSpec(memory_space=pltpu.VMEM)
        smem = pl.BlockSpec(memory_space=pltpu.SMEM)
        hbm = pl.BlockSpec(memory_space=pl.ANY)
        dma = pltpu.SemaphoreType.DMA
        return pl.pallas_call(
            functools.partial(layer_kernel, n_ctx, n_tp),
            out_shape=jax.ShapeDtypeStruct((length, width), BF16),
            in_specs=[vmem, vmem, vmem, vmem, vmem, smem, vmem, vmem, vmem, vmem, vmem, hbm],
            out_specs=vmem,
            scratch_shapes=[
                pltpu.VMEM((HALO, inner), BF16),
                pltpu.VMEM((2, HALO, size), BF16),
                pltpu.VMEM((2, length, size), BF16),
                pltpu.VMEM((HALO + length, inner), F32),
                pltpu.VMEM((HALO + length, 2 * size), F32),
                pltpu.VMEM((length, inner), F32),
                pltpu.VMEM((length, inner), F32),
                pltpu.VMEM((length, inner), F32),
                pltpu.VMEM((size, inner), BF16),
                pltpu.VMEM((8, inner), F32),
                pltpu.VMEM((n_ctx, size, inner), BF16),
                pltpu.VMEM((n_ctx, 8, inner), F32),
                pltpu.VMEM((size, inner), F32),
                pltpu.VMEM((n_tp, 8, length), F32),
                pltpu.VMEM((length, inner), BF16),
                pltpu.VMEM((length, inner), BF16),
                pltpu.VMEM((n_z, inner, width), BF16),
                pltpu.VMEM((n_z, inner, width), BF16),
                pltpu.VMEM((n_z, length, width), F32),
                pltpu.VMEM((n_z, length, width), BF16),
                pltpu.VMEM((n_z + 1, length, width), BF16),
                dma((4,)),
                dma((4,)),
                dma((2, n_ctx)),
                dma((2, n_ctx)),
                dma((n_tp,)),
                dma((n_tp,)),
                dma((2,)),
                dma((n_z,)),
                dma((n_z,)),
                dma((n_z,)),
                dma((n_z, CHUNKS)),
                dma((n_z + 1, CHUNKS)),
            ],
            compiler_params=pltpu.CompilerParams(
                collective_id=0, has_side_effects=True, vmem_limit_bytes=48 * 1024 * 1024
            ),
        )(
            x_input,
            z_input,
            bc_input,
            dt_input,
            decay_log.reshape(heads, 1),
            skip_weight.reshape(1, heads),
            conv_x,
            conv_bc,
            conv_bias_x.reshape(1, -1),
            conv_bias_bc.reshape(1, -1),
            norm_gain.reshape(1, -1),
            out_weight,
        )

    in_specs = (
        P("ctx", "tp"),
        P("ctx", "tp"),
        P("ctx", "tp"),
        P("ctx", "tp"),
        P("tp"),
        P("tp"),
        P(None, "tp"),
        P(),
        P("tp"),
        P(),
        P("tp"),
        P("tp", None),
    )
    return jax.shard_map(
        shards, mesh=mesh, in_specs=in_specs, out_specs=P("ctx", "tp"), check_vma=False
    )
```

time: 161 us -> 76.1 us (0.47)
  the two profiles are of different devices: /device:TPU:0 before, /device:TPU:22 now
where the time goes in v1:
time: 76.1 us; the launch traced here: 75.3 us
  Pallas kernels  66.1 us (87%)
  local copies, waits for them, and re-layouts  9.19 us (12%)
    pallas_call x1, Pallas kernels, shards(): pl.pallas_call(functools.partial(layer_kernel, n_ctx, n_tp), out_shape=ja...  66.1 us
    unnamed x20, local copies, waits for them, and re-layouts  8.47 us

profile of v1, /device:TPU:22, one launch (start us, length us, event | category | flops | bytes accessed | tf_op | source)
XLA Modules:
  0.0 75.3 jit_solution(16868680680906825430)
XLA Ops:
  0.0 0.7 copy.14.decay_ref
  0.7 0.8 %copy.13.dt_ref = f32[256,8]{1,0:T(8,128)S(1)} copy(f32[256,8]{0,1:T(8,128)} %param.15) | data formatting | bytes 16384 | tf_op args[3]
  1.6 0.0 copy-start
  1.6 0.9 %copy-done = bf16[256,512]{1,0:T(8,128)(2,1)S(1)} copy-done((bf16[256,512]{1,0:T(8,128)(2,1)S(1)}, bf16[256,512]{1,0:T(8,128)(2,1)}, u32[]{:S(2)}) %copy-start) | copy-done | bytes 262168
  2.5 0.0 copy-start.1
  2.5 0.9 %copy-done.1 = bf16[256,512]{1,0:T(8,128)(2,1)S(1)} copy-done((bf16[256,512]{1,0:T(8,128)(2,1)S(1)}, bf16[256,512]{1,0:T(8,128)(2,1)}, u32[]{:S(2)}) %copy-start.1) | copy-done | bytes 262168
  3.5 0.0 copy-start.2
  3.5 0.8 %copy-done.2 = bf16[256,128]{1,0:T(8,128)(2,1)S(1)} copy-done((bf16[256,128]{1,0:T(8,128)(2,1)S(1)}, bf16[256,128]{1,0:T(8,128)(2,1)}, u32[]{:S(2)}) %copy-start.2) | copy-done | bytes 65560
  4.3 0.0 copy-start.3
  4.3 0.7 copy-done.3
  5.0 0.0 copy-start.4
  5.0 0.7 copy-done.4
  5.7 0.0 copy-start.5
  5.7 0.7 copy-done.5
  6.4 0.0 copy-start.6
  6.4 0.7 copy-done.6
  7.1 0.0 copy-start.7
  7.1 0.7 copy-done.7
  7.8 0.0 copy-start.8
  7.8 0.7 copy-done.8
  8.4 66.1 %shard_map.118 = bf16[256,1024]{1,0:T(8,128)(2,1)S(1)} custom-call(bf16[256,512]{1,0:T(8,128)(2,1)S(1)} %copy-done, bf16[256,512]{1,0:T(8,128)(2,1)S(1)} %copy-done.1, bf16[256,128]{1,0:T(8,128)(2,1)S(1)} %copy-done.2, f32[256,8]{1,0:T(8,128)S(1)} %copy.13.dt_ref, f32[8,1]{1,0:T(8,128)S(1)} %copy.14.decay_ref, f32[1,8]{1,0:T(1,128)S(1)} %bitcast.8, ...), custom_call_target="tpu_custom_call" | custom-call | tf_op jit(solution)/shard_map/pallas_call | solution.py:469
  74.5 0.8 %copy.16 = bf16[256,1024]{1,0:T(8,128)(2,1)} copy(bf16[256,1024]{1,0:T(8,128)(2,1)S(1)} %shard_map.118) | data formatting | bytes 1048576
Async XLA Ops:
  1.6 1.0 %copy-start = (bf16[256,512]{1,0:T(8,128)(2,1)S(1)}, bf16[256,512]{1,0:T(8,128)(2,1)}, u32[]{:S(2)}) copy-start(bf16[256,512]{1,0:T(8,128)(2,1)} %x_ref.1) | copy-start | bytes 786436
  2.5 0.9 %copy-start.1 = (bf16[256,512]{1,0:T(8,128)(2,1)S(1)}, bf16[256,512]{1,0:T(8,128)(2,1)}, u32[]{:S(2)}) copy-start(bf16[256,512]{1,0:T(8,128)(2,1)} %z_ref.1) | copy-start | bytes 786436
  3.5 0.8 %copy-start.2 = (bf16[256,128]{1,0:T(8,128)(2,1)S(1)}, bf16[256,128]{1,0:T(8,128)(2,1)}, u32[]{:S(2)}) copy-start(bf16[256,128]{1,0:T(8,128)(2,1)} %bc_ref.1) | copy-start | bytes 196612
  4.3 0.7 copy-start.3
  5.0 0.7 copy-start.4
  5.7 0.7 copy-start.5
  6.4 0.7 copy-start.6
  7.1 0.7 copy-start.7
  7.8 0.7 copy-start.8

commit v2 on v1

--- a/solution.py
+++ b/solution.py
@@ -13,6 +13,7 @@
 BF16 = jnp.bfloat16
 HALO = 16
 CHUNKS = 4
+HALVES = 2
 
 
 def dot(a, b, precision=None):
@@ -31,9 +32,21 @@
 def layer_kernel(
     n_ctx,
     n_tp,
+    x_hbm,
+    z_hbm,
+    bc_ref,
+    dt_hbm,
+    decay_hbm,
+    skip_hbm,
+    conv_x_hbm,
+    conv_bc_hbm,
+    bias_x_hbm,
+    bias_bc_hbm,
+    gain_hbm,
+    w_ref,
+    out_ref,
     x_ref,
     z_ref,
-    bc_ref,
     dt_ref,
     decay_ref,
     skip_ref,
@@ -42,8 +55,7 @@
     bias_x_ref,
     bias_bc_ref,
     gain_ref,
-    w_ref,
-    out_ref,
+    fetch_sem,
     halo_x,
     halo_bc,
     raw_bc,
@@ -52,6 +64,8 @@
     xs,
     y,
     grown,
+    gate,
+    c_pair,
     state_own,
     carry_own,
     state_in,
@@ -71,7 +85,8 @@
     state_recv,
     square_send,
     square_recv,
-    hid_sem,
+    hid_send,
+    hid_recv,
     w_local,
     w_send,
     w_recv,
@@ -86,11 +101,30 @@
     n_z = n_tp // 2
     length, inner = x_ref.shape
     size = bc_ref.shape[1]
-    heads = dt_ref.shape[1]
+    heads = dt_ref.shape[0]
     taps = conv_x_ref.shape[0]
     width = w_own.shape[2]
     rows = length // CHUNKS
     wide = 2 * (inner // heads)
+
+    group = pl.ds(pl.multiple_of(zed * 2 * size, 2 * size), 2 * size)
+    fetched = {}
+    for at, (name, src, dst) in enumerate(
+        (
+            ("dt", dt_hbm, dt_ref),
+            ("decay", decay_hbm, decay_ref),
+            ("x", x_hbm, x_ref),
+            ("conv_x", conv_x_hbm, conv_x_ref),
+            ("bias_x", bias_x_hbm, bias_x_ref),
+            ("bc", bc_ref, raw_bc.at[core]),
+            ("conv_bc", conv_bc_hbm.at[:, group], conv_bc_ref),
+            ("bias_bc", bias_bc_hbm.at[:, group], bias_bc_ref),
+            ("skip", skip_hbm, skip_ref),
+            ("z", z_hbm, z_ref),
+            ("gain", gain_hbm, gain_ref),
+        )
+    ):
+        fetched[name] = pltpu.make_async_copy(src, dst, fetch_sem.at[at])
 
     barrier = pltpu.get_barrier_semaphore()
 
@@ -103,6 +137,9 @@
         greet(lax.rem(ctx + step, n_ctx), rank)
     greet(lax.rem(ctx + 1, n_ctx), sib)
     greet(lax.rem(ctx + n_ctx - 1, n_ctx), sib)
+
+    for copy in fetched.values():
+        copy.start()
 
     def w_block(block, half):
         return w_ref.at[:, pl.ds(pl.multiple_of((2 * block + half) * width, width), width)]
@@ -125,7 +162,7 @@
     later = lax.rem(ctx + 1, n_ctx)
     tail = pl.ds(length - HALO, HALO)
     x_halo = remote(
-        x_ref.at[tail], halo_x, halo_send.at[0], halo_recv.at[0], later, rank
+        x_hbm.at[tail], halo_x, halo_send.at[0], halo_recv.at[0], later, rank
     )
     bc_halo = remote(
         bc_ref.at[tail], halo_bc.at[core], halo_send.at[1], halo_recv.at[1 + core], later, rank
@@ -151,11 +188,15 @@
     for b in range(n_z):
         sent_w[b].start()
         local_w[b].start()
-    raw_bc[core] = bc_ref[...]
-
-    logits = dt_ref[...].T
+
+    fetched["dt"].wait()
+    fetched["decay"].wait()
+    logits = dt_ref[...]
     step_size = jnp.maximum(logits, 0.0) + jnp.log(1.0 + jnp.exp(-jnp.abs(logits)))
-    rate = -jnp.exp(decay_ref[...])
+    head_row = lax.broadcasted_iota(jnp.int32, (heads, heads), 0)
+    head_lane = lax.broadcasted_iota(jnp.int32, (heads, heads), 1)
+    decay = jnp.where(head_row == head_lane, decay_ref[...], 0.0)
+    rate = -jnp.exp(jnp.sum(decay, axis=1, keepdims=True))
     earlier = lax.broadcasted_iota(jnp.int32, (length, length), 0)
     after = lax.broadcasted_iota(jnp.int32, (length, length), 1)
     upper = jnp.where(earlier <= after, 1.0, 0.0).astype(F32)
@@ -180,6 +221,19 @@
         grown[:, at] = spread(grown_col, p)
         carry_own[:, at] = jnp.broadcast_to(spread(last_col, p), (8, wide))
 
+    def conv(pad, kernel, bias, begin, end):
+        value = bias
+        for k in range(taps):
+            start = HALO - (taps - 1) + k
+            value = value + kernel[k : k + 1, :] * pad[start + begin : start + end, :]
+        return silu(value)
+
+    fetched["x"].wait()
+    fetched["conv_x"].wait()
+    fetched["bias_x"].wait()
+    pad_x[HALO:, :] = x_ref[...].astype(F32)
+    xs[HALO:, :] = conv(pad_x, conv_x_ref[...], bias_x_ref[...], HALO, length)
+
     @pl.when(ctx == 0)
     def _():
         halo_x[...] = jnp.zeros_like(halo_x)
@@ -189,16 +243,8 @@
     def _():
         x_halo.wait_recv()
 
-    def conv(pad, kernel, bias):
-        value = bias
-        for k in range(taps):
-            start = HALO - (taps - 1) + k
-            value = value + kernel[k : k + 1, :] * pad[start : start + length, :]
-        return silu(value)
-
     pad_x[0:HALO, :] = halo_x[...].astype(F32)
-    pad_x[HALO:, :] = x_ref[...].astype(F32)
-    xs[...] = conv(pad_x, conv_x_ref[...], bias_x_ref[...])
+    xs[0:HALO, :] = conv(pad_x, conv_x_ref[...], bias_x_ref[...], 0, HALO)
 
     @pl.when(ctx > 0)
     def _():
@@ -207,13 +253,15 @@
                 halo_bc.at[half], halo_bc.at[half], halo_recv.at[1 + half]
             ).wait()
 
+    fetched["bc"].wait()
+    fetched["conv_bc"].wait()
+    fetched["bias_bc"].wait()
     bc_swap.wait_recv()
     for half in range(2):
         at = slice(half * size, (half + 1) * size)
         pad_bc[0:HALO, at] = halo_bc[half].astype(F32)
         pad_bc[HALO:, at] = raw_bc[half].astype(F32)
-    group = pl.ds(pl.multiple_of(zed * 2 * size, 2 * size), 2 * size)
-    bcs = conv(pad_bc, conv_bc_ref[:, group], bias_bc_ref[:, group])
+    bcs = conv(pad_bc, conv_bc_ref[...], bias_bc_ref[...], 0, length)
     b_mat = bcs[:, :size]
     c_mat = bcs[:, size:]
 
@@ -253,6 +301,8 @@
     meeting = lax.dot_general(
         c_mat, b_mat, (((1,), (1,)), ((), ())), preferred_element_type=F32, precision=HIGH
     )
+    fetched["skip"].wait()
+    skips = skip_ref[...]
     meeting = jnp.where(earlier >= after, meeting, 0.0)
     for p in range(pairs):
         at = slice(p * wide, (p + 1) * wide)
@@ -265,10 +315,12 @@
             weights = jnp.exp(jnp.minimum(gap, 0.0)) * meeting * step_size[h : h + 1, :]
             product = dot(weights.astype(BF16), both)
             parts.append(product[:, :wide] + product[:, wide:])
-        y[:, at] = jnp.where(first, parts[0], parts[1]) + values * jnp.where(
-            first, skip_ref[0, 2 * p], skip_ref[0, 2 * p + 1]
-        )
-    gate = silu(z_ref[...].astype(F32))
+        y[:, at] = jnp.where(first, parts[0], parts[1]) + values * spread(skips, p)
+    fetched["z"].wait()
+    fetched["gain"].wait()
+    c_high, c_low = split(c_mat)
+    c_pair[...] = jnp.concatenate([c_high, c_low], axis=1)
+    gate[...] = silu(z_ref[...].astype(F32))
 
     incoming[...] = jnp.zeros_like(incoming)
     for source in range(n_ctx - 1):
@@ -283,33 +335,24 @@
             ).wait()
             incoming[...] = incoming[...] * carry_in[source, 0:1, :] + state_in[source].astype(F32)
 
-    c_high, c_low = split(c_mat)
     state = incoming[...].astype(BF16)
-    carried = dot(
-        jnp.concatenate([c_high, c_low], axis=1), jnp.concatenate([state, state], axis=0)
-    )
-    gated = (y[...] + carried * grown[...]) * gate
-    hid_own[...] = (gated * gain_ref[...]).astype(BF16)
-    hid_swap = remote(hid_own, hid_sib, hid_sem.at[0], hid_sem.at[1], ctx, sib)
-    hid_swap.start()
-    norm = jnp.sum(gated * gated, axis=1, keepdims=True)
-    squares[rank] = jnp.broadcast_to(norm, (length, 128)).T[0:8, :]
-
-    def square_copy(target):
+    states = jnp.concatenate([state, state], axis=0)
+    half_rows = length // HALVES
+
+    def half(r):
+        return pl.ds(r * half_rows, half_rows)
+
+    def hid_swap(r):
         return remote(
-            squares.at[rank],
-            squares.at[rank],
-            square_send.at[target],
-            square_recv.at[rank],
-            ctx,
-            target,
-        )
-
-    for target in range(n_tp):
-
-        @pl.when(target != rank)
-        def _():
-            square_copy(target).start()
+            hid_own.at[half(r)], hid_sib.at[half(r)], hid_send.at[r], hid_recv.at[r], ctx, sib
+        )
+
+    for r in range(HALVES):
+        carried = dot(c_pair[half(r), :], states)
+        gated = (y[half(r), :] + carried * grown[half(r), :]) * gate[half(r), :]
+        y[half(r), :] = gated
+        hid_own[half(r), :] = (gated * gain_ref[...]).astype(BF16)
+        hid_swap(r).start()
 
     def part(r):
         return pl.ds(r * rows, rows)
@@ -336,29 +379,55 @@
     for b in range(n_z):
         local_w[b].wait()
         sent_w[b].wait_recv()
-    hid_swap.wait_recv()
+
+    def launch(target, chunks):
+        @pl.when((zed == 0) | (zed == n_z - 1))
+        def _():
+            for r in chunks:
+                outgoing[target, part(r)] = acc[target, part(r)].astype(BF16)
+
+        @pl.when(zed == 0)
+        def _():
+            for r in chunks:
+                block_copy(target, r, True).start()
+
+        @pl.when(zed == n_z - 1)
+        def _():
+            for r in chunks:
+                block_copy(target, r, False).start()
+
+    def square_copy(target):
+        return remote(
+            squares.at[rank],
+            squares.at[rank],
+            square_send.at[target],
+            square_recv.at[rank],
+            ctx,
+            target,
+        )
 
     upward = zed < n_z // 2
+    per_half = CHUNKS // HALVES
     for i in range(n_z):
         target = jnp.where(upward, n_z - 1 - i, i)
-        total_block = dot(hid_own[...], w_own[target]) + dot(hid_sib[...], w_sib[target])
-        acc[target] = total_block
-
-        if i < n_z - 1:
-
-            @pl.when((zed == 0) | (zed == n_z - 1))
-            def _():
-                outgoing[target] = acc[target].astype(BF16)
-
-            @pl.when(zed == 0)
-            def _():
-                for r in range(CHUNKS):
-                    block_copy(target, r, True).start()
-
-            @pl.when(zed == n_z - 1)
-            def _():
-                for r in range(CHUNKS):
-                    block_copy(target, r, False).start()
+        if i == 0:
+            for r in range(HALVES):
+                own = dot(hid_own[half(r), :], w_own[target])
+                hid_swap(r).wait_recv()
+                acc[target, half(r)] = own + dot(hid_sib[half(r), :], w_sib[target])
+                launch(target, range(r * per_half, (r + 1) * per_half))
+        else:
+            acc[target] = dot(hid_own[...], w_own[target]) + dot(hid_sib[...], w_sib[target])
+            if i < n_z - 1:
+                launch(target, range(CHUNKS))
+
+    norm = jnp.sum(y[...] * y[...], axis=1, keepdims=True)
+    squares[rank] = jnp.broadcast_to(norm, (length, 128)).T[0:8, :]
+    for target in range(n_tp):
+
+        @pl.when(target != rank)
+        def _():
+            square_copy(target).start()
 
     def relay(target, r, forward):
         block_wait(target, r)
@@ -420,7 +489,8 @@
             for copy in state_copies(target):
                 copy.wait_send()
 
-    hid_swap.wait_send()
+    for r in range(HALVES):
+        hid_swap(r).wait_send()
     for target in range(n_tp):
 
         @pl.when(target != rank)
@@ -463,15 +533,25 @@
         features = out_weight.shape[1]
         width = features // n_tp
         vmem = pl.BlockSpec(memory_space=pltpu.VMEM)
-        smem = pl.BlockSpec(memory_space=pltpu.SMEM)
         hbm = pl.BlockSpec(memory_space=pl.ANY)
         dma = pltpu.SemaphoreType.DMA
         return pl.pallas_call(
             functools.partial(layer_kernel, n_ctx, n_tp),
             out_shape=jax.ShapeDtypeStruct((length, width), BF16),
-            in_specs=[vmem, vmem, vmem, vmem, vmem, smem, vmem, vmem, vmem, vmem, vmem, hbm],
+            in_specs=[hbm] * 12,
             out_specs=vmem,
             scratch_shapes=[
+                pltpu.VMEM((length, inner), BF16),
+                pltpu.VMEM((length, inner), BF16),
+                pltpu.VMEM((heads, length), F32),
+                pltpu.VMEM((1, heads), F32),
+                pltpu.VMEM((1, heads), F32),
+                pltpu.VMEM((conv_x.shape[0], inner), F32),
+                pltpu.VMEM((conv_bc.shape[0], 2 * size), F32),
+                pltpu.VMEM((1, inner), F32),
+                pltpu.VMEM((1, 2 * size), F32),
+                pltpu.VMEM((1, inner), F32),
+                dma((11,)),
                 pltpu.VMEM((HALO, inner), BF16),
                 pltpu.VMEM((2, HALO, size), BF16),
                 pltpu.VMEM((2, length, size), BF16),
@@ -480,6 +560,8 @@
                 pltpu.VMEM((length, inner), F32),
                 pltpu.VMEM((length, inner), F32),
                 pltpu.VMEM((length, inner), F32),
+                pltpu.VMEM((length, inner), F32),
+                pltpu.VMEM((length, 2 * size), BF16),
                 pltpu.VMEM((size, inner), BF16),
                 pltpu.VMEM((8, inner), F32),
                 pltpu.VMEM((n_ctx, size, inner), BF16),
@@ -499,7 +581,8 @@
                 dma((2, n_ctx)),
                 dma((n_tp,)),
                 dma((n_tp,)),
-                dma((2,)),
+                dma((HALVES,)),
+                dma((HALVES,)),
                 dma((n_z,)),
                 dma((n_z,)),
                 dma((n_z,)),
@@ -507,14 +590,14 @@
                 dma((n_z + 1, CHUNKS)),
             ],
             compiler_params=pltpu.CompilerParams(
-                collective_id=0, has_side_effects=True, vmem_limit_bytes=48 * 1024 * 1024
+                collective_id=0, has_side_effects=True, vmem_limit_bytes=56 * 1024 * 1024
             ),
         )(
             x_input,
             z_input,
             bc_input,
-            dt_input,
-            decay_log.reshape(heads, 1),
+            dt_input.T,
+            decay_log.reshape(1, heads),
             skip_weight.reshape(1, heads),
             conv_x,
             conv_bc,

time: 76.1 us -> 68 us (0.89)
  local copies, waits for them, and re-layouts: 9.19 us -> 1.87 us
    unnamed x20 -> x1, local copies, waits for them, and re-layouts: 8.47 us -> 1.87 us
where the time goes in v2:
time: 68 us; the launch traced here: 67.8 us
  Pallas kernels  66 us (97%)
  local copies, waits for them, and re-layouts  1.87 us (3%)
    pallas_call x1, Pallas kernels, shards(): pl.pallas_call(functools.partial(layer_kernel, n_ctx, n_tp), out_shape=ja...  66 us
    unnamed x1, local copies, waits for them, and re-layouts  1.87 us

profile of v2, /device:TPU:22, one launch (start us, length us, event | category | flops | bytes accessed | tf_op | source)
XLA Modules:
  0.0 67.8 jit_solution(10182237976909692746)
XLA Ops:
  0.0 66.0 %shard_map.118 = bf16[256,1024]{1,0:T(8,128)(2,1)} custom-call(bf16[256,512]{1,0:T(8,128)(2,1)} %x_hbm.1, bf16[256,512]{1,0:T(8,128)(2,1)} %z_hbm.1, bf16[256,128]{1,0:T(8,128)(2,1)} %bc_ref.1, f32[8,256]{1,0:T(8,128)} %bitcast.6, f32[1,8]{1,0:T(1,128)} %bitcast.10, f32[1,8]{1,0:T(1,128)} %bitcast.11, f32[4,512]{1,0:T(4,128)} %conv_x_hbm.1, ...), custom_call_target="tpu_custom_call" | custom-call | tf_op jit(solution)/shard_map/pallas_call | solution.py:538
  66.0 1.9 %copy.14 = bf16[256,1024]{1,0:T(8,128)(2,1)} copy(bf16[256,1024]{1,0:T(8,128)(2,1)} %shard_map.118) | data formatting | bytes 1048576

commit v3 on v2

--- a/solution.py
+++ b/solution.py
@@ -92,6 +92,15 @@
     w_recv,
     block_send,
     block_recv,
+    w_lent,
+    hid_lent,
+    lend_send,
+    lend_recv,
+    spread_send,
+    spread_recv,
+    lent_send,
+    lent_recv,
+    pass_send,
 ):
     ctx = lax.axis_index("ctx")
     rank = lax.axis_index("tp")
@@ -188,6 +197,41 @@
     for b in range(n_z):
         sent_w[b].start()
         local_w[b].start()
+
+    lends = n_z >= 4
+    is_end = (zed == 0) | (zed == n_z - 1)
+    is_next = (zed == 1) | (zed == n_z - 2)
+    inner_zed = jnp.where(zed == 0, 1, n_z - 2)
+    share = inner // n_ctx
+    own_share = pl.ds(pl.multiple_of(ctx * share, share), share)
+
+    def lend_w(half):
+        columns = pl.ds(pl.multiple_of((2 * inner_zed + half) * width, width), width)
+        return remote(
+            w_ref.at[own_share, columns],
+            w_lent.at[core, own_share],
+            lend_send.at[half],
+            lend_recv.at[core],
+            ctx,
+            2 * inner_zed + half,
+        )
+
+    def spread_w(step):
+        return remote(
+            w_lent.at[:, own_share],
+            w_lent.at[:, own_share],
+            spread_send.at[step],
+            spread_recv.at[ctx],
+            lax.rem(ctx + step, n_ctx),
+            rank,
+        )
+
+    if lends:
+
+        @pl.when(is_end)
+        def _():
+            for half in range(2):
+                lend_w(half).start()
 
     fetched["dt"].wait()
     fetched["decay"].wait()
@@ -347,12 +391,53 @@
             hid_own.at[half(r)], hid_sib.at[half(r)], hid_send.at[r], hid_recv.at[r], ctx, sib
         )
 
+    def lend_hid(r):
+        return remote(
+            hid_own.at[half(r)],
+            hid_lent.at[core, half(r)],
+            lent_send.at[r],
+            lent_recv.at[core, r],
+            ctx,
+            2 * inner_zed + core,
+        )
+
+    def pass_hid(r):
+        return remote(
+            hid_lent.at[core, half(r)],
+            hid_lent.at[core, half(r)],
+            pass_send.at[r],
+            lent_recv.at[core, r],
+            ctx,
+            sib,
+        )
+
+    def lent_wait(source, r):
+        pltpu.make_async_copy(
+            hid_lent.at[source, half(r)], hid_lent.at[source, half(r)], lent_recv.at[source, r]
+        ).wait()
+
     for r in range(HALVES):
         carried = dot(c_pair[half(r), :], states)
         gated = (y[half(r), :] + carried * grown[half(r), :]) * gate[half(r), :]
         y[half(r), :] = gated
         hid_own[half(r), :] = (gated * gain_ref[...]).astype(BF16)
         hid_swap(r).start()
+        if lends:
+
+            @pl.when(is_end)
+            def _():
+                lend_hid(r).start()
+
+    if lends:
+
+        @pl.when(is_next)
+        def _():
+            for source in range(2):
+                pltpu.make_async_copy(
+                    w_lent.at[source, own_share], w_lent.at[source, own_share], lend_recv.at[source]
+                ).wait()
+            for step in range(1, n_ctx):
+                spread_w(step).start()
 
     def part(r):
         return pl.ds(r * rows, rows)
@@ -416,6 +501,12 @@
                 hid_swap(r).wait_recv()
                 acc[target, half(r)] = own + dot(hid_sib[half(r), :], w_sib[target])
                 launch(target, range(r * per_half, (r + 1) * per_half))
+        elif lends and i == n_z - 2:
+
+            @pl.when(jnp.logical_not(is_end))
+            def _():
+                acc[target] = dot(hid_own[...], w_own[target]) + dot(hid_sib[...], w_sib[target])
+
         else:
             acc[target] = dot(hid_own[...], w_own[target]) + dot(hid_sib[...], w_sib[target])
             if i < n_z - 1:
@@ -436,6 +527,14 @@
         ).astype(BF16)
         block_copy(target, r, forward).start()
 
+    if lends:
+
+        @pl.when(is_next)
+        def _():
+            for r in range(HALVES):
+                lent_wait(core, r)
+                pass_hid(r).start()
+
     for i in range(n_z - 1):
         for r in range(CHUNKS):
 
@@ -457,14 +556,35 @@
 
     mean = jnp.sum(squares[...], axis=0) * (1.0 / (inner * n_tp))
     scale = lax.rsqrt(mean + 1e-05).T[:, 0:1]
+    if lends:
+
+        @pl.when(is_next)
+        def _():
+            for r in range(HALVES):
+                lent_wait(1 - core, r)
+            for source in range(n_ctx):
+
+                @pl.when(source != ctx)
+                def _():
+                    rows_of = pl.ds(source * share, share)
+                    pltpu.make_async_copy(
+                        w_lent.at[:, rows_of], w_lent.at[:, rows_of], spread_recv.at[source]
+                    ).wait()
+
+            acc[zed] = acc[zed] + (
+                dot(hid_lent[0], w_lent[0]) + dot(hid_lent[1], w_lent[1])
+            )
+
+    from_above = (zed < n_z - 1) & (zed != n_z - 2) if lends else zed < n_z - 1
+    from_below = (zed > 0) & (zed != 1) if lends else zed > 0
     for r in range(CHUNKS):
 
-        @pl.when(zed < n_z - 1)
+        @pl.when(from_above)
         def _():
             block_wait(n_z, r)
             acc[zed, part(r)] = acc[zed, part(r)] + arrived[n_z, part(r)].astype(F32)
 
-        @pl.when(zed > 0)
+        @pl.when(from_below)
         def _():
             block_wait(zed, r)
             acc[zed, part(r)] = acc[zed, part(r)] + arrived[zed, part(r)].astype(F32)
@@ -497,10 +617,32 @@
         def _():
             square_copy(target).wait_send()
 
+    if lends:
+
+        @pl.when(is_end)
+        def _():
+            for half_at in range(2):
+                lend_w(half_at).wait_send()
+            for r in range(HALVES):
+                lend_hid(r).wait_send()
+
+        @pl.when(is_next)
+        def _():
+            for step in range(1, n_ctx):
+                spread_w(step).wait_send()
+            for r in range(HALVES):
+                pass_hid(r).wait_send()
+
     for target in range(n_z):
         for r in range(CHUNKS):
 
-            @pl.when(zed != target)
+            sent = zed != target
+            if lends and target == 1:
+                sent = sent & (zed != 0)
+            if lends and target == n_z - 2:
+                sent = sent & (zed != n_z - 1)
+
+            @pl.when(sent)
             def _():
                 pltpu.make_async_copy(
                     outgoing.at[target, part(r)],
@@ -588,6 +730,15 @@
                 dma((n_z,)),
                 dma((n_z, CHUNKS)),
                 dma((n_z + 1, CHUNKS)),
+                pltpu.VMEM((2, inner, width), BF16),
+                pltpu.VMEM((2, length, inner), BF16),
+                dma((2,)),
+                dma((2,)),
+                dma((n_ctx,)),
+                dma((n_ctx,)),
+                dma((HALVES,)),
+                dma((2, HALVES)),
+                dma((HALVES,)),
             ],
             compiler_params=pltpu.CompilerParams(
                 collective_id=0, has_side_effects=True, vmem_limit_bytes=56 * 1024 * 1024

time: 68 us -> 70.9 us (1.043)
  Pallas kernels: 66 us -> 68.9 us
    pallas_call x1, Pallas kernels: 66 us -> 68.9 us  [shards(): pl.pallas_call(functools.partial(layer_kernel, n_ctx, n_tp), out_shape=ja...]
where the time goes in v3:
time: 70.9 us; the launch traced here: 70.8 us
  Pallas kernels  68.9 us (97%)
  local copies, waits for them, and re-layouts  1.87 us (3%)
    pallas_call x1, Pallas kernels, shards(): pl.pallas_call(functools.partial(layer_kernel, n_ctx, n_tp), out_shape=ja...  68.9 us
    unnamed x1, local copies, waits for them, and re-layouts  1.87 us

profile of v3, /device:TPU:22, one launch (start us, length us, event | category | flops | bytes accessed | tf_op | source)
XLA Modules:
  0.0 70.8 jit_solution(8814986291344862122)
XLA Ops:
  0.0 68.9 %shard_map.118 = bf16[256,1024]{1,0:T(8,128)(2,1)} custom-call(bf16[256,512]{1,0:T(8,128)(2,1)} %x_hbm.1, bf16[256,512]{1,0:T(8,128)(2,1)} %z_hbm.1, bf16[256,128]{1,0:T(8,128)(2,1)} %bc_ref.1, f32[8,256]{1,0:T(8,128)} %bitcast.6, f32[1,8]{1,0:T(1,128)} %bitcast.10, f32[1,8]{1,0:T(1,128)} %bitcast.11, f32[4,512]{1,0:T(4,128)} %conv_x_hbm.1, ...), custom_call_target="tpu_custom_call" | custom-call | tf_op jit(solution)/shard_map/pallas_call | solution.py:680
  68.9 1.9 %copy.14 = bf16[256,1024]{1,0:T(8,128)(2,1)} copy(bf16[256,1024]{1,0:T(8,128)(2,1)} %shard_map.118) | data formatting | bytes 1048576
